TPU v7x, 256 devices: a whole 4x4x8 slice. The times are simulated.
256 devices in a mesh: rep: 16 (over x_hi, y, core), fsdp: 16 (over x_lo, z).
Axes of the slice: x: 4 (x_hi: 2, x_lo: 2; x = x_hi * 2 + x_lo), y: 4, z: 8, core: 2. Of those that a mesh axis runs over, the one named last changes fastest.
Arguments:
- activations: bfloat16 [65536, 8192], P(('rep', 'fsdp')), may hold values from -0.375 to 0.375
- cotangent: bfloat16 [65536, 512], P(('rep', 'fsdp')), may hold values from -6 to 6
- key_weight: bfloat16 [8192, 512], P('fsdp'), may hold values from -0.25 to 0.25
- momentum: float32 [16, 8192, 512], P('rep', 'fsdp'), may hold values from -6 to 6
- selection: int32 [16, 8192, 256], P('rep', 'fsdp'), may hold values from 0 to 63, as said below
Outputs:
- input_grad: bfloat16 [65536, 8192], P(('rep', 'fsdp'))
- new_momentum: float32 [16, 8192, 512], P('rep', 'fsdp')
- update: float32 [8192, 512], P('fsdp')
Inputs may be any that keep to these rules, and one draw needn't show every extreme that they name: `selection`: the 32 entries of one block name 32 different positions of that block of 64 values.
All inputs are finite; a program needn't handle non-finite values.
Results may differ from a plain program's by a relative error of at most 0.0075.
Values may be sent and summed in bfloat16 or wider, within the bound.
A program may use at most 128 MiB of HBM per device.

v0:
```python
import jax
import jax.numpy as jnp
from jax import lax
from jax.sharding import PartitionSpec as P

BLOCK = 64
KEEP = 32


decay_rate = 0.9


def cosine_table(columns):
    row_index = jnp.arange(columns, dtype=jnp.int32)[:, None]
    col_index = jnp.arange(columns, dtype=jnp.int32)[None, :]
    freq = (row_index % BLOCK).astype(jnp.float32)
    where_at = (col_index % BLOCK).astype(jnp.float32)
    base = jnp.sqrt(2.0 / BLOCK) * jnp.cos(jnp.pi * (2.0 * where_at + 1.0) * freq / (2.0 * BLOCK))
    base = jnp.where(row_index % BLOCK == 0, base * jnp.sqrt(0.5), base)
    return jnp.where(row_index // BLOCK == col_index // BLOCK, base, jnp.zeros_like(base))


def chosen_mask(selection, columns):
    row_count = selection.shape[0]
    groups = selection.reshape(row_count, columns // BLOCK, KEEP)
    hits = groups[..., None] == jnp.arange(BLOCK, dtype=jnp.int32)
    return jnp.any(hits, axis=2).reshape(row_count, columns)


def local(activations, cotangent, key_weight, momentum, selection):
    columns = key_weight.shape[1]
    contract_last = (((1,), (1,)), ((), ()))
    input_grad = lax.dot_general(
        cotangent,
        lax.all_gather(key_weight, "fsdp", axis=0, tiled=True),
        contract_last,
        preferred_element_type=jnp.float32,
    ).astype(jnp.bfloat16)
    gradient = lax.psum_scatter(
        lax.dot_general(
            activations, cotangent, (((0,), (0,)), ((), ())), preferred_element_type=jnp.float32
        ),
        "fsdp",
        scatter_dimension=0,
        tiled=True,
    )
    cosines = cosine_table(columns)
    blended = decay_rate * momentum[0] + gradient
    spectrum = jnp.dot(blended, cosines.T, precision=lax.Precision.HIGHEST)
    chosen = chosen_mask(selection[0], columns)
    retained = jnp.where(chosen, spectrum, jnp.zeros_like(spectrum))
    renewed = blended - jnp.dot(retained, cosines, precision=lax.Precision.HIGHEST)
    outgoing = retained.astype(jnp.bfloat16)
    replica_count = lax.axis_size("rep")
    gathered = lax.all_gather(outgoing[None], "rep", axis=0, tiled=True)
    summed = jnp.sum(gathered.astype(jnp.float32), axis=0)
    update = jnp.dot(summed, cosines, precision=lax.Precision.HIGHEST) / replica_count
    return (input_grad, renewed[None], update)


def solution(mesh):
    in_specs = (
        P(("rep", "fsdp"), None),
        P(("rep", "fsdp"), None),
        P("fsdp", None),
        P("rep", "fsdp", None),
        P("rep", "fsdp", None),
    )
    out_specs = (P(("rep", "fsdp"), None), P("rep", "fsdp", None), P("fsdp", None))
    return jax.shard_map(local, mesh=mesh, in_specs=in_specs, out_specs=out_specs, check_vma=False)
```

profile of v0, /device:TPU:1, one launch (start us, length us, event | category | flops | bytes accessed | tf_op | source)
XLA Modules:
  0.0 405.5 jit_solution(5388064861609116504)
XLA Ops:
  7.2 0.0 copy-start
  7.2 0.0 reduce-scatter.2.cloned.1.call-start
  7.2 0.9 copy-done
  8.1 10.3 %fusion.51 = f32[8192,512]{1,0:T(8,128)} fusion(bf16[256,8192]{1,0:T(8,128)(2,1)} %param.5, bf16[256,512]{1,0:T(8,128)(2,1)S(1)} %copy-done), kind=kOutput, calls=%fused_computation.65 | convolution fusion | flops 2147483648 | bytes 21233664 | tf_op jit(solution)/shard_map/dot_general | solution.py:40
  18.4 0.0 copy-start.4
  18.4 0.0 copy-start.1
  18.4 0.0 reduce-scatter.2.cloned.1.call-update
  18.4 0.0 all-gather.4.cloned.1.call-start
  18.5 0.7 all-gather.4.cloned.1.call-update
  19.2 0.2 all-gather.6.cloned.1.call-start
  19.4 0.0 copy-done.4
  19.5 0.2 copy.11
  19.7 7.8 %fusion = pred[512,8,64]{0,2,1:T(8,128)(4,1)S(1)} fusion(s32[512,8,32]{0,2,1:T(8,128)S(1)} %bitcast.20), kind=kLoop, calls=%fused_computation.1 | loop fusion | flops 16515072 | bytes 786432 | tf_op jit(solution)/shard_map/reduce_or | solution.py:27
  27.5 0.3 copy.12
  27.9 180.2 %reduce-scatter.2.cloned.1.call-done = f32[512,512]{1,0:T(8,128)} async-done(((f32[8192,512]{1,0:T(8,128)}), f32[512,512]{1,0:T(8,128)}) %reduce-scatter.2.cloned.1.call-update) | async-done | bytes 1048592 | tf_op jit(solution)/shard_map/reduce_scatter | solution.py:39
  208.1 0.0 copy-done.1
  208.1 0.0 copy-start.2
  208.1 8.3 %fusion.50 = (bf16[512,512]{1,0:T(8,128)(2,1)}, f32[512,512]{1,0:T(8,128)}) fusion(pred[512,512]{1,0:T(32,128)(4,1)S(1)} %copy.12, f32[512]{0:T(512)S(1)} %get-tuple-element.6, f32[512]{0:T(512)S(1)} %add_multiply_fusion, s32[512]{0:T(512)S(1)} %get-tuple-element.5, pred[512]{0:T(512)(128)(4,1)S(1)} %broadcast_compare_fusion, ...), kind=kOutput, calls=%fused_computation.64 | convolution fusion | flops 1613496320 | bytes 3938816 | tf_op jit(solution)/shard_map/dot_general | solution.py:49
  216.5 0.0 all-gather.6.cloned.1.call-update
  216.5 92.1 %all-gather.4.cloned.1.call-done = bf16[8192,512]{1,0:T(8,128)(2,1)} async-done(((bf16[512,512]{1,0:T(8,128)(2,1)}), bf16[8192,512]{1,0:T(8,128)(2,1)}) %all-gather.4.cloned.1.call-update) | async-done | bytes 8388624 | tf_op jit(solution)/shard_map/all_gather | solution.py:35
  308.7 0.0 copy-start.3
  308.7 7.9 %convolution_convert_fusion = bf16[256,8192]{1,0:T(8,128)(2,1)} fusion(bf16[256,512]{1,0:T(8,128)(2,1)S(1)} %copy-done, bf16[8192,512]{1,0:T(8,128)(2,1)} %all-gather.4.cloned.1.call-done), kind=kOutput, calls=%fused_computation.3 | convolution fusion | flops 2149580800 | bytes 12845056 | tf_op jit(solution)/shard_map/dot_general | solution.py:33
  316.5 0.0 copy-done.2
  316.5 0.0 copy-done.3
  316.5 6.7 %fusion.1 = f32[1,512,512]{2,1,0:T(8,128)} fusion(f32[512,512]{1,0:T(8,128)S(1)} %copy-done.3, f32[512]{0:T(512)S(1)} %get-tuple-element.6, f32[512]{0:T(512)S(1)} %add_multiply_fusion, s32[512]{0:T(512)S(1)} %get-tuple-element.5, pred[512]{0:T(512)(128)(4,1)S(1)} %broadcast_compare_fusion, f32[512,512]{1,0:T(8,128)S(1)} %copy-done.2, ...), kind=kOutput, calls=%fused_computation.6 | convolution fusion | flops 1613234176 | bytes 4200960 | tf_op jit(solution)/shard_map/dot_general | solution.py:52
  323.2 64.3 %all-gather.6.cloned.1.call-done = bf16[8192,512]{1,0:T(8,128)(2,1)} async-done(((bf16[512,512]{1,0:T(8,128)(2,1)}), bf16[8192,512]{1,0:T(8,128)(2,1)}) %all-gather.6.cloned.1.call-update) | async-done | bytes 8388624 | tf_op jit(solution)/shard_map/all_gather | solution.py:55
  387.6 4.7 %convert_reduce_fusion = f32[512,512]{1,0:T(8,128)S(1)} fusion(bf16[16,512,512]{2,1,0:T(8,128)(2,1)} %bitcast.19), kind=kLoop, calls=%fused_computation.2 | loop fusion | flops 8126464 | bytes 9437184 | tf_op jit(solution)/shard_map/reduce_sum | solution.py:56
  392.2 6.7 %convolution_multiply_fusion = f32[512,512]{1,0:T(8,128)} fusion(f32[512,512]{1,0:T(8,128)S(1)} %convert_reduce_fusion, f32[512]{0:T(512)S(1)} %get-tuple-element.6, f32[512]{0:T(512)S(1)} %add_multiply_fusion, s32[512]{0:T(512)S(1)} %get-tuple-element.5, pred[512]{0:T(512)(128)(4,1)S(1)} %broadcast_compare_fusion), kind=kOutput, calls=%fused_computation.4 | convolution fusion | flops 1612709888 | bytes 2103808 | tf_op jit(solution)/shard_map/dot_general | solution.py:57
  (3 shorter events, 0.0 us)
Async XLA Ops:
  7.2 1.0 copy-start
  7.2 201.0 %reduce-scatter.2.cloned.1.call-start = ((), (), s32[]{:S(2)}) async-start(), calls=%async_computation.2 | async-start | bytes 17825792 | tf_op jit(solution)/shard_map/reduce_scatter | solution.py:39
  18.4 1.0 copy-start.4
  18.4 189.7 %copy-start.1 = (f32[1,512,512]{2,1,0:T(8,128)S(1)}, f32[1,512,512]{2,1,0:T(8,128)}, u32[]{:S(2)}) copy-start(f32[1,512,512]{2,1,0:T(8,128)} %param.8) | copy-start | bytes 3145732
  18.4 290.2 %all-gather.4.cloned.1.call-start = ((), (), s32[]{:S(2)}) async-start(), calls=%async_computation.1 | async-start | bytes 8912896 | tf_op jit(solution)/shard_map/all_gather | solution.py:35
  19.2 368.4 %all-gather.6.cloned.1.call-start = ((), (), s32[]{:S(2)}) async-start(), calls=%async_computation.3 | async-start | bytes 8912896 | tf_op jit(solution)/shard_map/all_gather | solution.py:55
  208.1 108.4 %copy-start.2 = (f32[512,512]{1,0:T(8,128)S(1)}, f32[512,512]{1,0:T(8,128)}, u32[]{:S(2)}) copy-start(f32[512,512]{1,0:T(8,128)} %reduce-scatter.2.cloned.1.call-done) | copy-start | bytes 3145732
  308.7 7.9 %copy-start.3 = (f32[512,512]{1,0:T(8,128)S(1)}, f32[512,512]{1,0:T(8,128)}, u32[]{:S(2)}) copy-start(f32[512,512]{1,0:T(8,128)} %get-tuple-element.4) | copy-start | bytes 3145732
Sparse Core Ops, SparseCore 0:
  18.6 189.5 reduce-scatter.1
  209.9 98.6 all-gather.3
  311.4 76.1 all-gather.5
where the time goes:
time: 406 us; the launch traced here: 405 us
  waiting for transfers between devices  337 us (83%)
  matrix products  39.9 us (10%)
  between operations  13.8 us (3%)
  other arithmetic  12.5 us (3%)
    reduce_scatter x1, waiting for transfers between devices, local(): lax.psum_scatter(lax.dot_general(activations, cotangent, (((0,), (0,)), (...  180 us
    all_gather x1, waiting for transfers between devices, local(): lax.all_gather(key_weight, 'fsdp', axis=0, tiled=True)  92.1 us
    all_gather x1, waiting for transfers between devices, local(): gathered = lax.all_gather(outgoing[None], 'rep', axis=0, tiled=True)  64.3 us
    dot_general x1, matrix products, local(): lax.dot_general(activations, cotangent, (((0,), (0,)), ((), ())), preferr...  10.3 us
    dot_general x1, matrix products, local(): spectrum = jnp.dot(blended, cosines.T, precision=lax.Precision.HIGHEST)  8.35 us
  transfers between devices with their start and end apart: 3, of which 3 were waited for; matrix products, arithmetic and copies ran while one was open for 8% of the time, Pallas kernels for 0%

commit v1 on v0

v1 whole, which is shorter than its diff:
```python
import functools

import jax
import jax.numpy as jnp
import ml_dtypes
import numpy as np
from jax import lax
from jax.experimental import pallas as pl
from jax.experimental.pallas import tpu as pltpu
from jax.sharding import PartitionSpec as P

BLOCK = 64
KEEP = 32
DECAY = 0.9
MESH = pl.DeviceIdType.MESH
TOK = 256
D = 8192
KW = 512
SUB = 128
TILE = 256
ROUNDS = 2
RROWS = KW // ROUNDS
PIECE = RROWS // 8
f32, bf16 = jnp.float32, jnp.bfloat16


def cosine_tile():
    k = np.arange(BLOCK)[:, None].astype(np.float64)
    n = np.arange(BLOCK)[None, :].astype(np.float64)
    base = np.sqrt(2.0 / BLOCK) * np.cos(np.pi * (2.0 * n + 1.0) * k / (2.0 * BLOCK))
    base[0] *= np.sqrt(0.5)
    return np.kron(np.eye(TILE // BLOCK), base).astype(np.float32)


def split_np(a):
    hi = a.astype(ml_dtypes.bfloat16)
    lo = (a - hi.astype(np.float32)).astype(ml_dtypes.bfloat16)
    return np.stack([hi, lo])


def split(a):
    hi = a.astype(bf16)
    return hi, (a - hi.astype(f32)).astype(bf16)


def dot(a, b):
    return jnp.dot(a, b, preferred_element_type=f32)


def transform(a, table):
    hi, lo = split(a)
    t_hi, t_lo = table[0], table[1]
    parts = []
    for j in range(a.shape[1] // TILE):
        cols = slice(j * TILE, (j + 1) * TILE)
        parts.append(dot(hi[:, cols], t_hi) + (dot(lo[:, cols], t_hi) + dot(hi[:, cols], t_lo)))
    return parts[0] if len(parts) == 1 else jnp.concatenate(parts, axis=1)


def message(i):
    if i >= 28:
        return 0, i - 28
    sign, half = (1, 0) if i % 2 == 0 else (-1, 2)
    if i < 4:
        return 4, i // 2 + half
    stage, slot = (i - 4) // 8, ((i - 4) % 8) // 2
    if stage == 0 and sign > 0:
        slot = (slot + 2) % 4
    return sign * (3 - stage), slot


def kernel(
    x_ref, c_ref, w_ref, m_ref, s_ref, fwd_ref, inv_ref,
    ig_ref, nm_ref, u_ref,
    xb, cb, zs, zr, wg, igv, mv, sv, mk, out, nmv, uv, cx, pr, rb,
    x_ss, x_rs, x_ls, z_ss, z_rs, wa_ss, wa_rs, wb_ss, wb_rs, wc_ss, wc_rs,
    p_ss, p_rs, g_ss, g_rs, h_ss, h_rs, q_ss, q_rs, l_s, o_s,
):
    r, f = lax.axis_index("rep"), lax.axis_index("fsdp")
    xh, y, c, xl, z = r // 8, (r // 2) % 4, r % 2, f // 8, f % 8
    chip = xh * 4 + y
    piece = y * 2 + c

    def dev(xh=xh, y=y, c=c, xl=xl, z=z):
        return (xh * 8 + (y % 4) * 2 + c, xl * 8 + z % 8)

    x_mate = dev(xl=1 - xl)
    x_other = dev(xh=1 - xh, xl=1 - xl)
    core_mate = dev(c=1 - c)
    z_to = (dev(z=z + 1), dev(z=z + 7))
    chips = [dev(xh=(xh + k // 4) % 2, y=y + k % 4) for k in range(8)]
    peers = [x_mate, x_other, core_mate] + [dev(z=z + k) for k in range(1, 8)] + chips[1:]

    def send(src, dst, ss, rs, to):
        return pltpu.make_async_remote_copy(
            src_ref=src, dst_ref=dst, send_sem=ss, recv_sem=rs, device_id=to, device_id_type=MESH
        )

    barrier = pltpu.get_barrier_semaphore()
    for peer in peers:
        pl.semaphore_signal(barrier, inc=1, device_id=peer, device_id_type=MESH)
    pl.semaphore_wait(barrier, len(peers))

    c_send = send(c_ref, cb.at[pl.ds(TOK, TOK)], x_ss.at[32], x_rs.at[32], x_mate)
    c_send.start()

    def column(half, i):
        away, sub = message(i)
        return pl.multiple_of(half * (D // 2) + ((z + away + 8) % 8) * KW + sub * SUB, SUB)

    def x_send(i):
        return send(
            x_ref.at[:, pl.ds(column(1 - xl, i), SUB)], xb.at[i, pl.ds(TOK, TOK)], x_ss.at[i], x_rs.at[i], x_mate
        )

    def x_load(i):
        return pltpu.make_async_copy(
            x_ref.at[:, pl.ds(column(xl, i), SUB)], xb.at[i, pl.ds(0, TOK)], x_ls.at[i]
        )

    w_src = w_ref.at[pl.ds(pl.multiple_of(piece * 64, 64), 64)]
    wa = [
        send(w_src, wg.at[xl, z, piece], wa_ss.at[k - 1], wa_rs.at[k - 1], dev(z=z + k)) for k in range(1, 8)
    ]
    w_own = pltpu.make_async_copy(w_src, wg.at[xl, z, piece], l_s.at[0])
    c_own = pltpu.make_async_copy(c_ref, cb.at[pl.ds(0, TOK)], l_s.at[1])
    s_own = pltpu.make_async_copy(s_ref.at[0], sv, l_s.at[2])
    m_own = pltpu.make_async_copy(m_ref.at[0], mv, l_s.at[3])

    for i in range(4):
        x_send(i).start()
    for k in (0, 6, 1, 5, 2, 4, 3):
        wa[k].start()
    for i in range(4, 32):
        x_send(i).start()
    s_own.start()
    m_own.start()
    c_own.start()
    w_own.start()
    for i in range(32):
        x_load(i).start()

    s_own.wait()
    sel_row = lax.broadcasted_iota(jnp.int32, (KW // 2, KW), 0) // KEEP
    sel_col = lax.broadcasted_iota(jnp.int32, (KW // 2, KW), 1)
    spread = [
        jnp.where((sel_row == sel_col // BLOCK) & ((sel_col % BLOCK) // 16 == g), 1.0, 0.0).astype(bf16)
        for g in range(4)
    ]
    bit = lax.broadcasted_iota(jnp.int32, (SUB, KW), 1) % 16

    def mask_rows(b, carry):
        rows = pl.ds(pl.multiple_of(b * SUB, SUB), SUB)
        sel = sv[rows, :]
        power = jnp.left_shift(1, sel % 16).astype(f32)
        total = jnp.zeros((SUB, KW), f32)
        for g in range(4):
            total += dot(jnp.where(sel // 16 == g, power, 0.0).astype(bf16), spread[g])
        mk[rows, :] = (jnp.right_shift(total.astype(jnp.int32), bit) % 2).astype(f32)
        return carry

    lax.fori_loop(0, KW // SUB, mask_rows, 0)
    m_own.wait()
    c_own.wait()
    w_own.wait()

    def product(i):
        pltpu.make_async_copy(x_ref.at[:, pl.ds(0, SUB)], xb.at[i, pl.ds(0, TOK)], x_ls.at[i]).wait()
        send(xb.at[i, pl.ds(0, TOK)], xb.at[i, pl.ds(TOK, TOK)], x_ss.at[i], x_rs.at[i], x_mate).wait_recv()
        return lax.dot_general(xb[i], cb[...], (((0,), (0,)), ((), ())), preferred_element_type=f32)

    def z_copy(way, m):
        return send(zs.at[way, m], zr.at[way, m], z_ss.at[way, m], z_rs.at[way, m], z_to[way])

    def step(way, m, i, before):
        total = product(i)
        if before is not None:
            z_copy(way, before).wait_recv()
            total += zr[way, before].astype(f32)
        zs[way, m] = total.astype(bf16)
        z_copy(way, m).start()

    def steps(start, count, first, before):
        def body(k, carry):
            for way in range(2):
                step(way, first + k, start + 2 * k + way, None if before is None else before(way, k))
            return carry

        lax.fori_loop(0, count, body, 0)

    def group(x_side, y_side, core):
        return wg.at[x_side, :, (y_side % 4) * 2 + core]

    wb = [
        send(group(xl, y, c), group(xl, y, c), wb_ss.at[0], wb_rs.at[0], dev(y=y + 1)),
        send(group(xl, y, c), group(xl, y, c), wb_ss.at[1], wb_rs.at[1], dev(y=y + 3)),
        send(group(xl, y, c), group(xl, y, c), wb_ss.at[2], wb_rs.at[2], dev(y=y + 2)),
        send(group(xl, y, c), group(xl, y, c), wb_ss.at[3], wb_rs.at[3], x_other),
        send(group(xl, y + 3, c), group(xl, y + 3, c), wb_ss.at[4], wb_rs.at[4], x_other),
        send(group(1 - xl, y, c), group(1 - xl, y, c), wb_ss.at[5], wb_rs.at[5], dev(y=y + 3)),
        send(group(1 - xl, y + 3, c), group(1 - xl, y + 3, c), wb_ss.at[6], wb_rs.at[6], dev(y=y + 1)),
    ]
    groups = [(xl, y), (xl, y + 3), (xl, y + 1), (xl, y + 2), (1 - xl, y), (1 - xl, y + 3), (1 - xl, y + 1), (1 - xl, y + 2)]
    wc = [
        send(group(*g, c), group(*g, c), wc_ss.at[k], wc_rs.at[k], core_mate) for k, g in enumerate(groups)
    ]

    def input_grad(k):
        half, place = groups[k]
        place = place % 4
        wc[k].wait_recv()

        def body(zz, carry):
            rows = wg[half, zz, pl.ds(place * 2, 2)].reshape(SUB, KW)
            col = pl.multiple_of(half * (D // 2) + zz * KW + place * SUB, SUB)
            igv[:, pl.ds(col, SUB)] = lax.dot_general(
                cb[0:TOK], rows, (((1,), (1,)), ((), ())), preferred_element_type=f32
            ).astype(bf16)
            return carry

        lax.fori_loop(0, 8, body, 0)

    c_send.wait_recv()
    steps(0, 2, 0, None)
    for k in range(7):
        wa[k].wait_recv()
    for k in (3, 0, 1, 2):
        wb[k].start()
    wc[0].start()
    steps(4, 2, 2, None)
    steps(8, 2, 4, lambda way, k: k)
    input_grad(0)
    def at_two(way, k):
        return 2 + ((k + 2) % 4 if way == 0 else k)

    steps(12, 4, 6, at_two)
    wb[0].wait_recv()
    wb[3].wait_recv()
    wb[4].start()
    wb[5].start()
    wc[1].start()
    wc[4].start()
    wb[1].wait_recv()
    wc[2].start()
    input_grad(1)
    input_grad(4)
    input_grad(2)
    steps(20, 4, 10, lambda way, k: 6 + k)
    wb[4].wait_recv()
    wb[6].start()
    wb[2].wait_recv()
    wc[3].start()
    wc[5].start()

    def finish(b):
        rows = pl.ds(b * SUB, SUB)
        total = product(28 + b)
        z_copy(0, 10 + b).wait_recv()
        z_copy(1, 10 + b).wait_recv()
        total += zr[0, 10 + b].astype(f32) + zr[1, 10 + b].astype(f32)
        blended = DECAY * mv[rows, :] + total
        retained = mk[rows, :] * transform(blended, fwd_ref)
        out[rows, :] = retained.astype(bf16)
        nmv[rows, :] = blended - transform(retained, inv_ref)

    mine = pl.ds(pl.multiple_of(c * TILE, TILE), TILE)
    theirs = pl.ds(pl.multiple_of((1 - c) * TILE, TILE), TILE)

    def span(q):
        return pl.ds(q * RROWS, RROWS)

    def pair_copy(q):
        return send(out.at[span(q), theirs], cx.at[q], p_ss.at[q], p_rs.at[q], core_mate)

    def pieces(q, k):
        to = ((xh + k // 4) % 2) * 4 + (y + k) % 4
        return send(pr.at[q, to], rb.at[q, chip], g_ss.at[q, k - 1], g_rs.at[q, k - 1], chips[k])

    own_piece = [pl.ds(pl.multiple_of(q * RROWS + chip * PIECE, PIECE), PIECE) for q in range(ROUNDS)]

    def shares(q, k):
        at = uv.at[own_piece[q], mine]
        return send(at, at, h_ss.at[q, k - 1], h_rs.at[q, k - 1], chips[k])

    def halves(q):
        at = uv.at[span(q), mine]
        return send(at, at, q_ss.at[q], q_rs.at[q], core_mate)

    def scatter(q):
        pair_copy(q).wait_recv()
        both = out[span(q), mine].astype(f32) + cx[q].astype(f32)
        pr[q] = both.astype(bf16).reshape(8, PIECE, TILE)
        for k in range(1, 8):
            pieces(q, k).start()
        rb[q, chip] = pr[q, chip]

    def gather(q):
        for k in range(1, 8):
            pieces(q, k).wait_recv()
        summed = jnp.sum(rb[q].astype(f32), axis=0)
        uv[own_piece[q], mine] = transform(summed, inv_ref) * (1.0 / 16.0)
        for k in range(1, 8):
            shares(q, k).start()

    def exchange(q):
        for k in range(1, 8):
            shares(q, k).wait_recv()
        halves(q).start()

    u_out = [pltpu.make_async_copy(uv.at[span(q)], u_ref.at[span(q)], o_s.at[q]) for q in range(ROUNDS)]
    nm_out = pltpu.make_async_copy(nmv, nm_ref.at[0], o_s.at[ROUNDS])
    ig_out = pltpu.make_async_copy(igv, ig_ref, o_s.at[ROUNDS + 1])

    finish(0)
    finish(1)
    pair_copy(0).start()
    finish(2)
    scatter(0)
    finish(3)
    pair_copy(1).start()
    nm_out.start()
    wb[5].wait_recv()
    wc[6].start()
    wb[6].wait_recv()
    wc[7].start()
    scatter(1)
    input_grad(3)
    gather(0)
    input_grad(5)
    gather(1)
    input_grad(6)
    exchange(0)
    input_grad(7)
    ig_out.start()
    exchange(1)
    halves(0).wait_recv()
    u_out[0].start()
    halves(1).wait_recv()
    u_out[1].start()

    c_send.wait_send()
    for i in range(32):
        x_send(i).wait_send()

    def drain(m, carry):
        z_copy(0, m).wait_send()
        z_copy(1, m).wait_send()
        return carry

    lax.fori_loop(0, 14, drain, 0)
    for copy in wa + wb + wc:
        copy.wait_send()
    for q in range(ROUNDS):
        pair_copy(q).wait_send()
        halves(q).wait_send()
        for k in range(1, 8):
            pieces(q, k).wait_send()
            shares(q, k).wait_send()
        u_out[q].wait()
    nm_out.wait()
    ig_out.wait()


def local(activations, cotangent, key_weight, momentum, selection):
    table = cosine_tile()
    fwd, inv = split_np(np.ascontiguousarray(table.T)), split_np(table)
    hbm, vmem = pl.BlockSpec(memory_space=pl.ANY), pl.BlockSpec(memory_space=pltpu.VMEM)
    dma = pltpu.SemaphoreType.DMA
    return pl.pallas_call(
        kernel,
        out_shape=(
            jax.ShapeDtypeStruct((TOK, D), bf16),
            jax.ShapeDtypeStruct((1, KW, KW), f32),
            jax.ShapeDtypeStruct((KW, KW), f32),
        ),
        in_specs=[hbm] * 5 + [vmem] * 2,
        out_specs=(hbm, hbm, hbm),
        scratch_shapes=[
            pltpu.VMEM((32, 2 * TOK, SUB), bf16),
            pltpu.VMEM((2 * TOK, KW), bf16),
            pltpu.VMEM((2, 14, SUB, KW), bf16),
            pltpu.VMEM((2, 14, SUB, KW), bf16),
            pltpu.VMEM((2, 8, 8, 64, KW), bf16),
            pltpu.VMEM((TOK, D), bf16),
            pltpu.VMEM((KW, KW), f32),
            pltpu.VMEM((KW, KW // 2), jnp.int32),
            pltpu.VMEM((KW, KW), f32),
            pltpu.VMEM((KW, KW), bf16),
            pltpu.VMEM((KW, KW), f32),
            pltpu.VMEM((KW, KW), f32),
            pltpu.VMEM((ROUNDS, RROWS, TILE), bf16),
            pltpu.VMEM((ROUNDS, 8, PIECE, TILE), bf16),
            pltpu.VMEM((ROUNDS, 8, PIECE, TILE), bf16),
            dma((33,)), dma((33,)), dma((32,)),
            dma((2, 14)), dma((2, 14)),
            dma((7,)), dma((7,)), dma((7,)), dma((7,)), dma((8,)), dma((8,)),
            dma((ROUNDS,)), dma((ROUNDS,)),
            dma((ROUNDS, 7)), dma((ROUNDS, 7)), dma((ROUNDS, 7)), dma((ROUNDS, 7)),
            dma((ROUNDS,)), dma((ROUNDS,)),
            dma((4,)), dma((ROUNDS + 2,)),
        ],
        compiler_params=pltpu.CompilerParams(
            collective_id=0, has_side_effects=True, vmem_limit_bytes=48 << 20
        ),
        name="demo_step",
    )(activations, cotangent, key_weight, momentum, selection, jnp.asarray(fwd), jnp.asarray(inv))


def solution(mesh):
    in_specs = (
        P(("rep", "fsdp"), None),
        P(("rep", "fsdp"), None),
        P("fsdp", None),
        P("rep", "fsdp", None),
        P("rep", "fsdp", None),
    )
    out_specs = (P(("rep", "fsdp"), None), P("rep", "fsdp", None), P("fsdp", None))
    return jax.shard_map(local, mesh=mesh, in_specs=in_specs, out_specs=out_specs, check_vma=False)
```

time: 406 us -> 102 us (0.25)
  waiting for transfers between devices: 337 us -> 0 us
  Pallas kernels: 0 us -> 87.9 us
  matrix products: 39.9 us -> 0 us
  between operations: 13.8 us -> 0.65 us
  other arithmetic: 12.5 us -> 0 us
  local copies, waits for them, and re-layouts: 1.49 us -> 12.7 us
    reduce_scatter x1 -> x0, waiting for transfers between devices: 180 us -> none  [local(): lax.psum_scatter(lax.dot_general(activations, cotangent, (((0,), (0,)), (...]
    all_gather x2 -> x0, waiting for transfers between devices: 156 us -> none  [the longest x1 92.1 us: local(): lax.all_gather(key_weight, 'fsdp', axis=0, tiled=True)]
    pallas_call x0 -> x1, Pallas kernels: none -> 87.9 us  [local(): pl.pallas_call(kernel, out_shape=(jax.ShapeDtypeStruct((TOK, D), bf16), j...]
    dot_general x5 -> x0, matrix products: 39.9 us -> none  [the longest x1 10.3 us: local(): lax.dot_general(activations, cotangent, (((0,), (0,)), ((), ())), preferr...]
    unnamed x11 -> x15, local copies, waits for them, and re-layouts: 1.14 us -> 12.7 us
    reduce_or x1 -> x0, other arithmetic: 7.83 us -> none  [chosen_mask(): return jnp.any(hits, axis=2).reshape(row_count, columns)]
    reduce_sum x1 -> x0, other arithmetic: 4.65 us -> none  [local(): summed = jnp.sum(gathered.astype(jnp.float32), axis=0)]
  transfers between devices with their start and end apart: 3 -> 0, of which waited for: 3 -> 0; matrix products, arithmetic and copies ran while one was open for 8% -> 0% of each run, Pallas kernels for 0% -> 0%
where the time goes in v1:
time: 102 us; the launch traced here: 101 us
  Pallas kernels  87.9 us (86%)
  local copies, waits for them, and re-layouts  12.7 us (12%)
    pallas_call x1, Pallas kernels, local(): pl.pallas_call(kernel, out_shape=(jax.ShapeDtypeStruct((TOK, D), bf16), j...  87.9 us
    unnamed x15, local copies, waits for them, and re-layouts  12.7 us

profile of v1, /device:TPU:1, one launch (start us, length us, event | category | flops | bytes accessed | tf_op | source)
XLA Modules:
  0.0 101.3 jit_solution(3993762749628463832)
XLA Ops:
  0.6 0.0 copy-start
  0.6 1.2 %copy-done = f32[1,512,512]{2,1,0:T(8,128)S(1)} copy-done((f32[1,512,512]{2,1,0:T(8,128)S(1)}, f32[1,512,512]{2,1,0:T(8,128)}, u32[]{:S(2)}) %copy-start) | copy-done | bytes 1048600
  1.9 0.0 copy-start.1
  1.9 1.0 %copy-done.1 = bf16[512,512]{1,0:T(8,128)(2,1)S(1)} copy-done((bf16[512,512]{1,0:T(8,128)(2,1)S(1)}, bf16[512,512]{1,0:T(8,128)(2,1)}, u32[]{:S(2)}) %copy-start.1) | copy-done | bytes 524312
  2.9 0.0 copy-start.2
  2.9 1.0 %copy-done.2 = s32[1,512,256]{2,1,0:T(8,128)S(1)} copy-done((s32[1,512,256]{2,1,0:T(8,128)S(1)}, s32[1,512,256]{2,1,0:T(8,128)}, u32[]{:S(2)}) %copy-start.2) | copy-done | bytes 524312
  3.9 0.0 copy-start.3
  3.9 0.9 copy-done.3
  4.9 0.0 copy-start.4
  4.9 0.9 copy-done.4
  5.8 0.0 copy-start.5
  5.8 0.9 copy-done.5
  6.8 87.9 %demo_step.1 = (bf16[256,8192]{1,0:T(8,128)(2,1)}, f32[1,512,512]{2,1,0:T(8,128)S(1)}, f32[512,512]{1,0:T(8,128)S(1)}) custom-call(bf16[256,8192]{1,0:T(8,128)(2,1)} %x_ref.1, bf16[256,512]{1,0:T(8,128)(2,1)S(1)} %copy-done.3, bf16[512,512]{1,0:T(8,128)(2,1)S(1)} %copy-done.1, f32[1,512,512]{2,1,0:T(8,128)S(1)} %copy-done, s32[1,512,256]{2,1,0:T(8,128)S(1)} %copy-done.2, ...), custom_call_target="tpu_custom_call" | custom-call | tf_op jit(solution)/shard_map/demo_step/pallas_call | solution.py:369
  94.7 4.6 %copy.13 = bf16[256,8192]{1,0:T(8,128)(2,1)} copy(bf16[256,8192]{1,0:T(8,128)(2,1)} %get-tuple-element.6) | data formatting | bytes 8388608
  99.3 1.0 copy.14
  100.3 1.0 copy.15
Async XLA Ops:
  0.6 1.2 %copy-start = (f32[1,512,512]{2,1,0:T(8,128)S(1)}, f32[1,512,512]{2,1,0:T(8,128)}, u32[]{:S(2)}) copy-start(f32[1,512,512]{2,1,0:T(8,128)} %m_ref.1) | copy-start | bytes 3145732
  1.9 1.0 %copy-start.1 = (bf16[512,512]{1,0:T(8,128)(2,1)S(1)}, bf16[512,512]{1,0:T(8,128)(2,1)}, u32[]{:S(2)}) copy-start(bf16[512,512]{1,0:T(8,128)(2,1)} %w_ref.1) | copy-start | bytes 1572868
  2.9 1.0 %copy-start.2 = (s32[1,512,256]{2,1,0:T(8,128)S(1)}, s32[1,512,256]{2,1,0:T(8,128)}, u32[]{:S(2)}) copy-start(s32[1,512,256]{2,1,0:T(8,128)} %s_ref.1) | copy-start | bytes 1572868
  3.9 0.9 copy-start.3
  4.9 0.9 copy-start.4
  5.8 0.9 copy-start.5

commit v2 on v1

v2 whole, which is shorter than its diff:
```python
import functools

import jax
import jax.numpy as jnp
import numpy as np
from jax import lax
from jax.experimental import pallas as pl
from jax.experimental.pallas import tpu as pltpu
from jax.sharding import PartitionSpec as P

BLOCK = 64
KEEP = 32
DECAY = 0.9
MESH = pl.DeviceIdType.MESH
TOK = 256
D = 8192
KW = 512
SUB = 128
TILE = 256
ROUNDS = 4
RROWS = KW // ROUNDS
PIECE = RROWS // 8
VMEM_LIMIT = 44 << 20
FLUSH_LIMIT = 1 << 20
f32, bf16 = jnp.float32, jnp.bfloat16


def cosine_tile(flip):
    row = lax.broadcasted_iota(jnp.int32, (TILE, TILE), 1 if flip else 0)
    col = lax.broadcasted_iota(jnp.int32, (TILE, TILE), 0 if flip else 1)
    freq, where_at = row % BLOCK, col % BLOCK
    angle = ((2 * where_at + 1) * freq) % (4 * BLOCK)
    base = (2.0 / BLOCK) ** 0.5 * jnp.cos(angle.astype(f32) * (np.pi / (2 * BLOCK)))
    base = jnp.where(freq == 0, base * 0.5**0.5, base)
    return jnp.where(row // BLOCK == col // BLOCK, base, 0.0)


def split(a):
    hi = a.astype(bf16)
    return hi, (a - hi.astype(f32)).astype(bf16)


def dot(a, b):
    return jnp.dot(a, b, preferred_element_type=f32)


def transform(a, table):
    hi, lo = split(a)
    t_hi, t_lo = table[0], table[1]
    parts = []
    for j in range(a.shape[1] // TILE):
        cols = slice(j * TILE, (j + 1) * TILE)
        parts.append(dot(hi[:, cols], t_hi) + (dot(lo[:, cols], t_hi) + dot(hi[:, cols], t_lo)))
    return parts[0] if len(parts) == 1 else jnp.concatenate(parts, axis=1)


def message(i):
    if i < 4:
        return 4, i // 2 + 2 * (i % 2)
    if i < 20:
        sign, stage, slot = 1 - 2 * (i % 2), (i - 4) // 8, ((i - 4) % 8) // 2
        if stage == 0 and sign > 0:
            slot = (slot + 2) % 4
        return sign * (3 - stage), slot
    return [(1, 0), (-1, 0), (1, 1), (-1, 1), (0, 0), (1, 2), (-1, 2), (0, 1), (1, 3), (-1, 3), (0, 2), (0, 3)][i - 20]


OWN = [next(i for i in range(32) if message(i) == (0, b)) for b in range(4)]
SUMS = [
    (0, None, None), (2, None, None), (4, None, None), (6, None, None), (8, 0, 0), (10, 1, 1), (12, 4, 2),
    (14, 5, 3), (16, 2, 4), (18, 3, 5), (20, 6, 6), (22, 7, 7), (25, 8, 8), (28, 9, 9),
]


def kernel(
    x_ref, c_ref, w_ref, m_ref, s_ref,
    ig_ref, nm_ref, u_ref,
    xb, cb, zs, zr, wg, mv, sv, mk, out, cx, pr, rb, sb, fwd_ref, inv_ref,
    x_ss, x_rs, x_ls, z_ss, z_rs, wa_ss, wa_rs, wb_ss, wb_rs, wd_ss, wd_rs, wc_ss, wc_rs,
    p_ss, p_rs, g_ss, g_rs, h_ss, h_rs, q_ss, q_rs, l_s,
):
    r, f = lax.axis_index("rep"), lax.axis_index("fsdp")
    xh, y, c, xl, z = r // 8, (r // 2) % 4, r % 2, f // 8, f % 8
    chip = xh * 4 + y
    piece = y * 2 + c

    def dev(xh=xh, y=y, c=c, xl=xl, z=z):
        return (xh * 8 + (y % 4) * 2 + c, xl * 8 + z % 8)

    x_mate = dev(xl=1 - xl)
    x_other = dev(xh=1 - xh, xl=1 - xl)
    core_mate = dev(c=1 - c)
    z_to = (dev(z=z + 1), dev(z=z + 7))
    chips = [dev(xh=(xh + k // 4) % 2, y=y + k % 4) for k in range(8)]
    peers = [x_mate, x_other, core_mate, *z_to] + chips[1:]

    def send(src, dst, ss, rs, to):
        return pltpu.make_async_remote_copy(
            src_ref=src, dst_ref=dst, send_sem=ss, recv_sem=rs, device_id=to, device_id_type=MESH
        )

    barrier = pltpu.get_barrier_semaphore()
    for peer in peers:
        pl.semaphore_signal(barrier, inc=1, device_id=peer, device_id_type=MESH)
    pl.semaphore_wait(barrier, len(peers))

    c_send = send(c_ref, cb.at[pl.ds(TOK, TOK)], x_ss.at[32], x_rs.at[32], x_mate)
    c_send.start()

    def column(half, i):
        away, sub = message(i)
        return pl.multiple_of(half * (D // 2) + ((z + away + 8) % 8) * KW + sub * SUB, SUB)

    def x_send(i):
        return send(
            x_ref.at[:, pl.ds(column(1 - xl, i), SUB)], xb.at[i, pl.ds(TOK, TOK)], x_ss.at[i], x_rs.at[i], x_mate
        )

    def x_load(i):
        return pltpu.make_async_copy(
            x_ref.at[:, pl.ds(column(xl, i), SUB)], xb.at[i, pl.ds(0, TOK)], x_ls.at[i]
        )

    w_src = w_ref.at[pl.ds(pl.multiple_of(piece * 64, 64), 64)]
    w_own = pltpu.make_async_copy(w_src, wg.at[xl, z, piece], l_s.at[0])
    c_own = pltpu.make_async_copy(c_ref, cb.at[pl.ds(0, TOK)], l_s.at[1])
    s_own = pltpu.make_async_copy(s_ref.at[0], sv, l_s.at[2])
    m_own = pltpu.make_async_copy(m_ref.at[0], mv, l_s.at[3])

    def ring(way, s):
        slot = wg.at[xl, (z + (8 - s if way == 0 else s)) % 8, piece]
        src = w_src if s == 0 else slot
        return send(src, slot, wa_ss.at[way, s], wa_rs.at[way, s], z_to[way])

    in_plane = (dev(y=y + 1), dev(y=y + 3), x_other)

    def plane(k, n):
        slot = wg.at[xl, (z + 8 - n) % 8, piece]
        return send(w_src if n == 0 else slot, slot, wb_ss.at[k, n], wb_rs.at[k, n], in_plane[k])

    def pass_on(way, s):
        ring(way, s).wait_recv()
        if s < (3 if way == 0 else 2):
            ring(way, s + 1).start()
        for k in range(3):
            plane(k, s + 1 if way == 0 else 7 - s).start()

    for i in range(2):
        x_send(i).start()
    ring(0, 0).start()
    ring(1, 0).start()
    for k in range(3):
        plane(k, 0).start()
    for i in range(2, 32):
        x_send(i).start()
    s_own.start()
    w_own.start()
    c_own.start()
    for i in range(32):
        x_load(i).start()
    m_own.start()
    pass_on(0, 0)
    pass_on(1, 0)

    s_own.wait()
    sel_row = lax.broadcasted_iota(jnp.int32, (KW // 2, KW), 0) // KEEP
    sel_col = lax.broadcasted_iota(jnp.int32, (KW // 2, KW), 1)
    spread = [
        jnp.where((sel_row == sel_col // BLOCK) & ((sel_col % BLOCK) // 16 == g), 1.0, 0.0).astype(bf16)
        for g in range(4)
    ]
    bit = lax.broadcasted_iota(jnp.int32, (SUB, KW), 1) % 16

    def mask_rows(b, carry):
        rows = pl.ds(pl.multiple_of(b * SUB, SUB), SUB)
        sel = sv[rows, :]
        power = jnp.left_shift(1, sel % 16).astype(f32)
        total = jnp.zeros((SUB, KW), f32)
        for g in range(4):
            total += dot(jnp.where(sel // 16 == g, power, 0.0).astype(bf16), spread[g])
        mk[rows, :] = (jnp.right_shift(total.astype(jnp.int32), bit) % 2).astype(f32)
        return carry

    lax.fori_loop(0, KW // SUB, mask_rows, 0)
    pass_on(0, 1)
    pass_on(1, 1)
    fwd_ref[0], fwd_ref[1] = split(cosine_tile(True))
    inv_ref[0], inv_ref[1] = split(cosine_tile(False))
    w_own.wait()
    c_own.wait()
    m_own.wait()

    def product(i):
        pltpu.make_async_copy(x_ref.at[:, pl.ds(0, SUB)], xb.at[i, pl.ds(0, TOK)], x_ls.at[i]).wait()
        send(xb.at[i, pl.ds(0, TOK)], xb.at[i, pl.ds(TOK, TOK)], x_ss.at[i], x_rs.at[i], x_mate).wait_recv()
        return lax.dot_general(xb[i], cb[...], (((0,), (0,)), ((), ())), preferred_element_type=f32)

    def z_copy(way, m):
        return send(zs.at[way, m], zr.at[way, m], z_ss.at[way, m], z_rs.at[way, m], z_to[way])

    def step(way, m, i, before):
        total = product(i)
        if before is not None:
            z_copy(way, before).wait_recv()
            total += zr[way, before].astype(f32)
        zs[way, m] = total.astype(bf16)
        z_copy(way, m).start()

    def steps(m):
        first, *before = SUMS[m]
        for way in range(2):
            step(way, m, first + way, before[way])

    def group(x_side, y_side, core):
        return wg.at[x_side, :, (y_side % 4) * 2 + core]

    def later(n, at, to):
        return send(at, at, wd_ss.at[n], wd_rs.at[n], to)

    def half_group(x_side, y_side, h):
        return wg.at[x_side, pl.ds(4 * h, 4), (y_side % 4) * 2 + c]

    wd = [
        later(0, group(xl, y, c), dev(y=y + 2)),
        later(1, group(1 - xl, y, c), dev(y=y + 3)),
        later(2, half_group(xl, y + 3, 0), x_other),
        later(3, half_group(xl, y + 3, 1), x_other),
        later(4, half_group(1 - xl, y + 3, 0), dev(y=y + 1)),
        later(5, half_group(1 - xl, y + 3, 1), dev(y=y + 1)),
    ]
    groups = [(xl, y), (xl, y + 3), (xl, y + 1), (1 - xl, y), (xl, y + 2), (1 - xl, y + 3), (1 - xl, y + 1), (1 - xl, y + 2)]
    wc = [
        send(group(*g, c), group(*g, c), wc_ss.at[k], wc_rs.at[k], core_mate) for k, g in enumerate(groups)
    ]

    def input_grad(k):
        half, place = groups[k]
        place = place % 4
        wc[k].wait_recv()

        def body(zz, carry):
            rows = wg[half, zz, pl.ds(place * 2, 2)].reshape(SUB, KW)
            col = pl.multiple_of(half * (D // 2) + zz * KW + place * SUB, SUB)
            ig_ref[:, pl.ds(col, SUB)] = lax.dot_general(
                cb[0:TOK], rows, (((1,), (1,)), ((), ())), preferred_element_type=f32
            ).astype(bf16)
            return carry

        lax.fori_loop(0, 8, body, 0)

    mine = pl.ds(pl.multiple_of(c * TILE, TILE), TILE)
    theirs = pl.ds(pl.multiple_of((1 - c) * TILE, TILE), TILE)
    span = [pl.ds(q * RROWS, RROWS) for q in range(ROUNDS)]
    own_piece = [pl.ds(pl.multiple_of(q * RROWS + chip * PIECE, PIECE), PIECE) for q in range(ROUNDS)]

    def pair(q):
        return send(out.at[span[q], theirs], cx.at[q], p_ss.at[q], p_rs.at[q], core_mate)

    def pieces(q, k):
        to = ((xh + k // 4) % 2) * 4 + (y + k) % 4
        return send(pr.at[q, to], rb.at[q, chip], g_ss.at[q, k - 1], g_rs.at[q, k - 1], chips[k])

    def shares(q, k):
        at = sb.at[own_piece[q], mine]
        return send(at, at, h_ss.at[q, k - 1], h_rs.at[q, k - 1], chips[k])

    def halves(q):
        at = sb.at[span[q], mine]
        return send(at, at, q_ss.at[q], q_rs.at[q], core_mate)

    def finish(b):
        rows = pl.ds(b * SUB, SUB)
        total = product(OWN[b]) + DECAY * mv[rows, :]
        z_copy(0, 10 + b).wait_recv()
        z_copy(1, 10 + b).wait_recv()
        total += zr[0, 10 + b].astype(f32) + zr[1, 10 + b].astype(f32)
        retained = mk[rows, :] * transform(total, fwd_ref)
        out[rows, :] = retained.astype(bf16)
        pair(b).start()
        nm_ref[rows, :] = total
        mk[rows, :] = retained

    def renew(b):
        rows = pl.ds(b * SUB, SUB)
        nm_ref[rows, :] -= transform(mk[rows, :], inv_ref)

    def scatter(q):
        pair(q).wait_recv()
        both = out[span[q], mine].astype(f32) + cx[q].astype(f32)
        pr[q] = both.astype(bf16).reshape(8, PIECE, TILE)
        for k in range(1, 8):
            pieces(q, k).start()

    def gather(q):
        rb[q, chip] = pr[q, chip]
        for k in range(1, 8):
            pieces(q, k).wait_recv()
        sb[own_piece[q], mine] = jnp.sum(rb[q].astype(f32), axis=0).astype(bf16)
        for k in range(1, 8):
            shares(q, k).start()

    def exchange(q):
        for k in range(1, 8):
            shares(q, k).wait_recv()
        halves(q).start()

    def result(q):
        halves(q).wait_recv()
        both = sb[span[q], :]
        for j in range(KW // TILE):
            cols = slice(j * TILE, (j + 1) * TILE)
            u_ref[span[q], cols] = (dot(both[:, cols], inv_ref[0]) + dot(both[:, cols], inv_ref[1])) * (1.0 / 16.0)

    c_send.wait_recv()
    steps(0)
    pass_on(0, 2)
    pass_on(1, 2)
    steps(1)
    steps(2)
    pass_on(0, 3)
    wd[0].start()
    wc[0].start()
    steps(3)
    input_grad(0)
    steps(4)
    for k in range(3):
        for n in range(8):
            plane(k, n).wait_recv()
    for k in (2, 3, 1):
        wd[k].start()
    for k in (3, 1, 2):
        wc[k].start()
    steps(5)
    input_grad(3)
    steps(6)
    input_grad(1)
    steps(7)
    wd[2].wait_recv()
    wd[4].start()
    steps(8)
    input_grad(2)
    steps(9)
    wd[3].wait_recv()
    wd[5].start()
    wc[5].start()
    wd[0].wait_recv()
    wc[4].start()
    steps(10)
    input_grad(5)
    steps(11)
    input_grad(4)
    finish(0)
    steps(12)
    wd[1].wait_recv()
    wc[6].start()
    finish(1)
    steps(13)
    finish(2)
    scatter(0)
    scatter(1)
    finish(3)
    scatter(2)
    wd[4].wait_recv()
    wd[5].wait_recv()
    wc[7].start()
    scatter(3)
    gather(0)
    gather(1)
    input_grad(6)
    gather(2)
    gather(3)
    renew(0)
    renew(1)
    exchange(0)
    exchange(1)
    input_grad(7)
    exchange(2)
    renew(2)
    renew(3)
    exchange(3)
    for q in range(ROUNDS):
        result(q)

    c_send.wait_send()
    for i in range(32):
        x_send(i).wait_send()

    def drain(m, carry):
        z_copy(0, m).wait_send()
        z_copy(1, m).wait_send()
        return carry

    lax.fori_loop(0, 14, drain, 0)
    for s in range(4):
        ring(0, s).wait_send()
    for s in range(3):
        ring(1, s).wait_send()
    for k in range(3):
        for n in range(8):
            plane(k, n).wait_send()
    for copy in wd + wc:
        copy.wait_send()
    for q in range(ROUNDS):
        pair(q).wait_send()
        halves(q).wait_send()
        for k in range(1, 8):
            pieces(q, k).wait_send()
            shares(q, k).wait_send()


def flush(ig_ref, nm_ref, u_ref, ig_out, nm_out, u_out, sems):
    copies = [
        pltpu.make_async_copy(ig_ref.at[pl.ds(k * 64, 64)], ig_out.at[pl.ds(k * 64, 64)], sems.at[k]) for k in range(4)
    ]
    copies += [pltpu.make_async_copy(nm_ref, nm_out.at[0], sems.at[4]), pltpu.make_async_copy(u_ref, u_out, sems.at[5])]
    for copy in copies:
        copy.start()
    for copy in copies:
        copy.wait()


def local(activations, cotangent, key_weight, momentum, selection):
    hbm, vmem = pl.BlockSpec(memory_space=pltpu.HBM), pl.BlockSpec(memory_space=pltpu.VMEM)
    dma = pltpu.SemaphoreType.DMA
    outs = pl.pallas_call(
        kernel,
        out_shape=(
            jax.ShapeDtypeStruct((TOK, D), bf16),
            jax.ShapeDtypeStruct((KW, KW), f32),
            jax.ShapeDtypeStruct((KW, KW), f32),
        ),
        in_specs=[hbm] * 5,
        out_specs=(vmem, vmem, vmem),
        scratch_shapes=[
            pltpu.VMEM((32, 2 * TOK, SUB), bf16),
            pltpu.VMEM((2 * TOK, KW), bf16),
            pltpu.VMEM((2, 14, SUB, KW), bf16),
            pltpu.VMEM((2, 14, SUB, KW), bf16),
            pltpu.VMEM((2, 8, 8, 64, KW), bf16),
            pltpu.VMEM((KW, KW), f32),
            pltpu.VMEM((KW, KW // 2), jnp.int32),
            pltpu.VMEM((KW, KW), f32),
            pltpu.VMEM((KW, KW), bf16),
            pltpu.VMEM((ROUNDS, RROWS, TILE), bf16),
            pltpu.VMEM((ROUNDS, 8, PIECE, TILE), bf16),
            pltpu.VMEM((ROUNDS, 8, PIECE, TILE), bf16),
            pltpu.VMEM((KW, KW), bf16),
            pltpu.VMEM((2, TILE, TILE), bf16),
            pltpu.VMEM((2, TILE, TILE), bf16),
            dma((33,)), dma((33,)), dma((32,)),
            dma((2, 14)), dma((2, 14)),
            dma((2, 4)), dma((2, 4)), dma((3, 8)), dma((3, 8)), dma((6,)), dma((6,)), dma((8,)), dma((8,)),
            dma((ROUNDS,)), dma((ROUNDS,)),
            dma((ROUNDS, 7)), dma((ROUNDS, 7)), dma((ROUNDS, 7)), dma((ROUNDS, 7)),
            dma((ROUNDS,)), dma((ROUNDS,)), dma((4,)),
        ],
        compiler_params=pltpu.CompilerParams(
            collective_id=0, has_side_effects=True, vmem_limit_bytes=VMEM_LIMIT
        ),
        name="demo_step",
    )(*(pltpu.with_memory_space_constraint(a, pltpu.HBM) for a in (activations, cotangent, key_weight, momentum, selection)))
    return pl.pallas_call(
        flush,
        out_shape=(
            jax.ShapeDtypeStruct((TOK, D), bf16),
            jax.ShapeDtypeStruct((1, KW, KW), f32),
            jax.ShapeDtypeStruct((KW, KW), f32),
        ),
        in_specs=[vmem] * 3,
        out_specs=(hbm, hbm, hbm),
        scratch_shapes=[dma((6,))],
        compiler_params=pltpu.CompilerParams(vmem_limit_bytes=FLUSH_LIMIT),
        name="flush",
    )(*outs)


def solution(mesh):
    in_specs = (
        P(("rep", "fsdp"), None),
        P(("rep", "fsdp"), None),
        P("fsdp", None),
        P("rep", "fsdp", None),
        P("rep", "fsdp", None),
    )
    out_specs = (P(("rep", "fsdp"), None), P("rep", "fsdp", None), P("fsdp", None))
    return jax.shard_map(local, mesh=mesh, in_specs=in_specs, out_specs=out_specs, check_vma=False)
```

time: 102 us -> 86.6 us (0.85)
  local copies, waits for them, and re-layouts: 12.7 us -> 0 us
  Pallas kernels: 87.9 us -> 85.9 us
    unnamed x15 -> x0, local copies, waits for them, and re-layouts: 12.7 us -> none
    pallas_call x1, Pallas kernels: 87.9 us -> 83.2 us  [local(): pl.pallas_call(kernel, out_shape=(jax.ShapeDtypeStruct((TOK, D), bf16), j...]
    pallas_call x0 -> x1, Pallas kernels: none -> 2.72 us  [local(): pl.pallas_call(flush, out_shape=(jax.ShapeDtypeStruct((TOK, D), bf16), ja...]
where the time goes in v2:
time: 86.6 us; the launch traced here: 86.5 us
  Pallas kernels  85.9 us (99%)
    pallas_call x1, Pallas kernels, local(): pl.pallas_call(kernel, out_shape=(jax.ShapeDtypeStruct((TOK, D), bf16), j...  83.2 us
    pallas_call x1, Pallas kernels, local(): pl.pallas_call(flush, out_shape=(jax.ShapeDtypeStruct((TOK, D), bf16), ja...  2.72 us

profile of v2, /device:TPU:1, one launch (start us, length us, event | category | flops | bytes accessed | tf_op | source)
XLA Modules:
  0.0 86.5 jit_solution(10868995092022862928)
XLA Ops:
  0.6 83.2 %demo_step.1 = (bf16[256,8192]{1,0:T(8,128)(2,1)S(1)}, f32[512,512]{1,0:T(8,128)S(1)}, f32[512,512]{1,0:T(8,128)S(1)}) custom-call(bf16[256,8192]{1,0:T(8,128)(2,1)} %x_ref.1, bf16[256,512]{1,0:T(8,128)(2,1)} %c_ref.1, bf16[512,512]{1,0:T(8,128)(2,1)} %w_ref.1, f32[1,512,512]{2,1,0:T(8,128)} %m_ref.1, s32[1,512,256]{2,1,0:T(8,128)} %s_ref.1), custom_call_target="tpu_custom_call" | custom-call | tf_op jit(solution)/shard_map/demo_step/pallas_call | solution.py:425
  83.8 2.7 %flush.1 = (bf16[256,8192]{1,0:T(8,128)(2,1)}, f32[1,512,512]{2,1,0:T(8,128)}, f32[512,512]{1,0:T(8,128)}) custom-call(bf16[256,8192]{1,0:T(8,128)(2,1)S(1)} %get-tuple-element.6.ig_ref, f32[512,512]{1,0:T(8,128)S(1)} %get-tuple-element.7.nm_ref, f32[512,512]{1,0:T(8,128)S(1)} %get-tuple-element.8.u_ref), custom_call_target="tpu_custom_call" | custom-call | tf_op jit(solution)/shard_map/flush/pallas_call | solution.py:462

commit v3 on v2

--- a/solution.py
+++ b/solution.py
@@ -62,13 +62,13 @@
         if stage == 0 and sign > 0:
             slot = (slot + 2) % 4
         return sign * (3 - stage), slot
-    return [(1, 0), (-1, 0), (1, 1), (-1, 1), (0, 0), (1, 2), (-1, 2), (0, 1), (1, 3), (-1, 3), (0, 2), (0, 3)][i - 20]
+    return [(1, 0), (-1, 0), (1, 1), (-1, 1), (1, 2), (-1, 2), (1, 3), (-1, 3), (0, 0), (0, 1), (0, 2), (0, 3)][i - 20]
 
 
 OWN = [next(i for i in range(32) if message(i) == (0, b)) for b in range(4)]
 SUMS = [
     (0, None, None), (2, None, None), (4, None, None), (6, None, None), (8, 0, 0), (10, 1, 1), (12, 4, 2),
-    (14, 5, 3), (16, 2, 4), (18, 3, 5), (20, 6, 6), (22, 7, 7), (25, 8, 8), (28, 9, 9),
+    (14, 5, 3), (16, 2, 4), (18, 3, 5), (20, 6, 6), (22, 7, 7), (24, 8, 8), (26, 9, 9),
 ]
 
 
@@ -238,15 +238,14 @@
         place = place % 4
         wc[k].wait_recv()
 
-        def body(zz, carry):
-            rows = wg[half, zz, pl.ds(place * 2, 2)].reshape(SUB, KW)
-            col = pl.multiple_of(half * (D // 2) + zz * KW + place * SUB, SUB)
-            ig_ref[:, pl.ds(col, SUB)] = lax.dot_general(
+        for first in range(0, 8, 4):
+            rows = wg[half, pl.ds(first, 4), pl.ds(place * 2, 2)].reshape(4 * SUB, KW)
+            grads = lax.dot_general(
                 cb[0:TOK], rows, (((1,), (1,)), ((), ())), preferred_element_type=f32
             ).astype(bf16)
-            return carry
-
-        lax.fori_loop(0, 8, body, 0)
+            for n in range(4):
+                col = pl.multiple_of(half * (D // 2) + (first + n) * KW + place * SUB, SUB)
+                ig_ref[:, pl.ds(col, SUB)] = grads[:, n * SUB : (n + 1) * SUB]
 
     mine = pl.ds(pl.multiple_of(c * TILE, TILE), TILE)
     theirs = pl.ds(pl.multiple_of((1 - c) * TILE, TILE), TILE)
@@ -349,14 +348,14 @@
     input_grad(5)
     steps(11)
     input_grad(4)
-    finish(0)
     steps(12)
+    steps(13)
     wd[1].wait_recv()
     wc[6].start()
+    finish(0)
     finish(1)
-    steps(13)
+    scatter(0)
     finish(2)
-    scatter(0)
     scatter(1)
     finish(3)
     scatter(2)
@@ -364,26 +363,23 @@
     wd[5].wait_recv()
     wc[7].start()
     scatter(3)
+    c_send.wait_send()
+    for i in range(32):
+        x_send(i).wait_send()
+    for s in range(4):
+        ring(0, s).wait_send()
+    for s in range(3):
+        ring(1, s).wait_send()
     gather(0)
     gather(1)
+    for k in range(3):
+        for n in range(8):
+            plane(k, n).wait_send()
     input_grad(6)
     gather(2)
     gather(3)
     renew(0)
     renew(1)
-    exchange(0)
-    exchange(1)
-    input_grad(7)
-    exchange(2)
-    renew(2)
-    renew(3)
-    exchange(3)
-    for q in range(ROUNDS):
-        result(q)
-
-    c_send.wait_send()
-    for i in range(32):
-        x_send(i).wait_send()
 
     def drain(m, carry):
         z_copy(0, m).wait_send()
@@ -391,21 +387,34 @@
         return carry
 
     lax.fori_loop(0, 14, drain, 0)
-    for s in range(4):
-        ring(0, s).wait_send()
-    for s in range(3):
-        ring(1, s).wait_send()
-    for k in range(3):
-        for n in range(8):
-            plane(k, n).wait_send()
-    for copy in wd + wc:
+    for copy in wd:
+        copy.wait_send()
+    exchange(0)
+    exchange(1)
+    input_grad(7)
+    renew(2)
+    renew(3)
+    for copy in wc:
         copy.wait_send()
     for q in range(ROUNDS):
         pair(q).wait_send()
+        for k in range(1, 8):
+            pieces(q, k).wait_send()
+    exchange(2)
+    result(0)
+    result(1)
+    for q in range(2):
+        for k in range(1, 8):
+            shares(q, k).wait_send()
+    exchange(3)
+    result(2)
+    for k in range(1, 8):
+        shares(2, k).wait_send()
+    result(3)
+    for k in range(1, 8):
+        shares(3, k).wait_send()
+    for q in range(ROUNDS):
         halves(q).wait_send()
-        for k in range(1, 8):
-            pieces(q, k).wait_send()
-            shares(q, k).wait_send()
 
 
 def flush(ig_ref, nm_ref, u_ref, ig_out, nm_out, u_out, sems):

time: 86.6 us -> 81.6 us (0.942)
  Pallas kernels: 85.9 us -> 80.8 us
    pallas_call x1, Pallas kernels: 83.2 us -> 78.1 us  [local(): pl.pallas_call(kernel, out_shape=(jax.ShapeDtypeStruct((TOK, D), bf16), j...]
where the time goes in v3:
time: 81.6 us; the launch traced here: 81.5 us
  Pallas kernels  80.8 us (99%)
    pallas_call x1, Pallas kernels, local(): pl.pallas_call(kernel, out_shape=(jax.ShapeDtypeStruct((TOK, D), bf16), j...  78.1 us
    pallas_call x1, Pallas kernels, local(): pl.pallas_call(flush, out_shape=(jax.ShapeDtypeStruct((TOK, D), bf16), ja...  2.72 us

profile of v3, /device:TPU:1, one launch (start us, length us, event | category | flops | bytes accessed | tf_op | source)
XLA Modules:
  0.0 81.5 jit_solution(17250379624834399033)
XLA Ops:
  0.6 78.1 %demo_step.1 = (bf16[256,8192]{1,0:T(8,128)(2,1)S(1)}, f32[512,512]{1,0:T(8,128)S(1)}, f32[512,512]{1,0:T(8,128)S(1)}) custom-call(bf16[256,8192]{1,0:T(8,128)(2,1)} %x_ref.1, bf16[256,512]{1,0:T(8,128)(2,1)} %c_ref.1, bf16[512,512]{1,0:T(8,128)(2,1)} %w_ref.1, f32[1,512,512]{2,1,0:T(8,128)} %m_ref.1, s32[1,512,256]{2,1,0:T(8,128)} %s_ref.1), custom_call_target="tpu_custom_call" | custom-call | tf_op jit(solution)/shard_map/demo_step/pallas_call | solution.py:434
  78.8 2.7 %flush.1 = (bf16[256,8192]{1,0:T(8,128)(2,1)}, f32[1,512,512]{2,1,0:T(8,128)}, f32[512,512]{1,0:T(8,128)}) custom-call(bf16[256,8192]{1,0:T(8,128)(2,1)S(1)} %get-tuple-element.6.ig_ref, f32[512,512]{1,0:T(8,128)S(1)} %get-tuple-element.7.nm_ref, f32[512,512]{1,0:T(8,128)S(1)} %get-tuple-element.8.u_ref), custom_call_target="tpu_custom_call" | custom-call | tf_op jit(solution)/shard_map/flush/pallas_call | solution.py:471

commit v4 on v3

--- a/solution.py
+++ b/solution.py
@@ -17,9 +17,8 @@
 KW = 512
 SUB = 128
 TILE = 256
-ROUNDS = 4
-RROWS = KW // ROUNDS
-PIECE = RROWS // 8
+ROUNDS = ((0, 2), (2, 1), (3, 1))
+N_ROUNDS = len(ROUNDS)
 VMEM_LIMIT = 44 << 20
 FLUSH_LIMIT = 1 << 20
 f32, bf16 = jnp.float32, jnp.bfloat16
@@ -65,6 +64,7 @@
     return [(1, 0), (-1, 0), (1, 1), (-1, 1), (1, 2), (-1, 2), (1, 3), (-1, 3), (0, 0), (0, 1), (0, 2), (0, 3)][i - 20]
 
 
+FAR = (6, 5, 7, 4, 2, 1, 3)
 OWN = [next(i for i in range(32) if message(i) == (0, b)) for b in range(4)]
 SUMS = [
     (0, None, None), (2, None, None), (4, None, None), (6, None, None), (8, 0, 0), (10, 1, 1), (12, 4, 2),
@@ -249,15 +249,21 @@
 
     mine = pl.ds(pl.multiple_of(c * TILE, TILE), TILE)
     theirs = pl.ds(pl.multiple_of((1 - c) * TILE, TILE), TILE)
-    span = [pl.ds(q * RROWS, RROWS) for q in range(ROUNDS)]
-    own_piece = [pl.ds(pl.multiple_of(q * RROWS + chip * PIECE, PIECE), PIECE) for q in range(ROUNDS)]
+    span = [pl.ds(first * SUB, count * SUB) for first, count in ROUNDS]
+
+    def piece_of(q, j):
+        first, count = ROUNDS[q]
+        return pl.ds(pl.multiple_of(first * SUB + j * (count * SUB // 8), 16), count * SUB // 8)
+
+    own_piece = [piece_of(q, chip) for q in range(N_ROUNDS)]
+    closing = {first + count - 1: q for q, (first, count) in enumerate(ROUNDS)}
 
     def pair(q):
-        return send(out.at[span[q], theirs], cx.at[q], p_ss.at[q], p_rs.at[q], core_mate)
+        return send(out.at[span[q], theirs], cx.at[span[q]], p_ss.at[q], p_rs.at[q], core_mate)
 
     def pieces(q, k):
         to = ((xh + k // 4) % 2) * 4 + (y + k) % 4
-        return send(pr.at[q, to], rb.at[q, chip], g_ss.at[q, k - 1], g_rs.at[q, k - 1], chips[k])
+        return send(pr.at[piece_of(q, to)], rb.at[own_piece[q]], g_ss.at[q, k - 1], g_rs.at[q, k - 1], chips[k])
 
     def shares(q, k):
         at = sb.at[own_piece[q], mine]
@@ -275,7 +281,8 @@
         total += zr[0, 10 + b].astype(f32) + zr[1, 10 + b].astype(f32)
         retained = mk[rows, :] * transform(total, fwd_ref)
         out[rows, :] = retained.astype(bf16)
-        pair(b).start()
+        if b in closing:
+            pair(closing[b]).start()
         nm_ref[rows, :] = total
         mk[rows, :] = retained
 
@@ -285,17 +292,17 @@
 
     def scatter(q):
         pair(q).wait_recv()
-        both = out[span[q], mine].astype(f32) + cx[q].astype(f32)
-        pr[q] = both.astype(bf16).reshape(8, PIECE, TILE)
-        for k in range(1, 8):
+        both = out[span[q], mine].astype(f32) + cx[span[q], :].astype(f32)
+        pr[span[q], :] = both.astype(bf16)
+        for k in FAR:
             pieces(q, k).start()
 
     def gather(q):
-        rb[q, chip] = pr[q, chip]
+        rb[own_piece[q], :] = pr[own_piece[q], :]
         for k in range(1, 8):
             pieces(q, k).wait_recv()
-        sb[own_piece[q], mine] = jnp.sum(rb[q].astype(f32), axis=0).astype(bf16)
-        for k in range(1, 8):
+        sb[own_piece[q], mine] = jnp.sum(rb[span[q], :].astype(f32).reshape(8, -1, TILE), axis=0).astype(bf16)
+        for k in FAR:
             shares(q, k).start()
 
     def exchange(q):
@@ -354,15 +361,15 @@
     wc[6].start()
     finish(0)
     finish(1)
+    finish(2)
     scatter(0)
-    finish(2)
+    finish(3)
     scatter(1)
-    finish(3)
     scatter(2)
     wd[4].wait_recv()
     wd[5].wait_recv()
     wc[7].start()
-    scatter(3)
+    gather(0)
     c_send.wait_send()
     for i in range(32):
         x_send(i).wait_send()
@@ -370,16 +377,15 @@
         ring(0, s).wait_send()
     for s in range(3):
         ring(1, s).wait_send()
-    gather(0)
-    gather(1)
     for k in range(3):
         for n in range(8):
             plane(k, n).wait_send()
     input_grad(6)
+    renew(0)
+    gather(1)
+    renew(1)
     gather(2)
-    gather(3)
-    renew(0)
-    renew(1)
+    renew(2)
 
     def drain(m, carry):
         z_copy(0, m).wait_send()
@@ -390,30 +396,26 @@
     for copy in wd:
         copy.wait_send()
     exchange(0)
-    exchange(1)
     input_grad(7)
-    renew(2)
     renew(3)
     for copy in wc:
         copy.wait_send()
-    for q in range(ROUNDS):
+    for q in range(N_ROUNDS):
         pair(q).wait_send()
         for k in range(1, 8):
             pieces(q, k).wait_send()
+    exchange(1)
+    result(0)
+    for k in range(1, 8):
+        shares(0, k).wait_send()
+    for k in range(1, 8):
+        shares(1, k).wait_send()
     exchange(2)
-    result(0)
     result(1)
-    for q in range(2):
-        for k in range(1, 8):
-            shares(q, k).wait_send()
-    exchange(3)
-    result(2)
     for k in range(1, 8):
         shares(2, k).wait_send()
-    result(3)
-    for k in range(1, 8):
-        shares(3, k).wait_send()
-    for q in range(ROUNDS):
+    result(2)
+    for q in range(N_ROUNDS):
         halves(q).wait_send()
 
 
@@ -450,18 +452,18 @@
             pltpu.VMEM((KW, KW // 2), jnp.int32),
             pltpu.VMEM((KW, KW), f32),
             pltpu.VMEM((KW, KW), bf16),
-            pltpu.VMEM((ROUNDS, RROWS, TILE), bf16),
-            pltpu.VMEM((ROUNDS, 8, PIECE, TILE), bf16),
-            pltpu.VMEM((ROUNDS, 8, PIECE, TILE), bf16),
+            pltpu.VMEM((KW, TILE), bf16),
+            pltpu.VMEM((KW, TILE), bf16),
+            pltpu.VMEM((KW, TILE), bf16),
             pltpu.VMEM((KW, KW), bf16),
             pltpu.VMEM((2, TILE, TILE), bf16),
             pltpu.VMEM((2, TILE, TILE), bf16),
             dma((33,)), dma((33,)), dma((32,)),
             dma((2, 14)), dma((2, 14)),
             dma((2, 4)), dma((2, 4)), dma((3, 8)), dma((3, 8)), dma((6,)), dma((6,)), dma((8,)), dma((8,)),
-            dma((ROUNDS,)), dma((ROUNDS,)),
-            dma((ROUNDS, 7)), dma((ROUNDS, 7)), dma((ROUNDS, 7)), dma((ROUNDS, 7)),
-            dma((ROUNDS,)), dma((ROUNDS,)), dma((4,)),
+            dma((N_ROUNDS,)), dma((N_ROUNDS,)),
+            dma((N_ROUNDS, 7)), dma((N_ROUNDS, 7)), dma((N_ROUNDS, 7)), dma((N_ROUNDS, 7)),
+            dma((N_ROUNDS,)), dma((N_ROUNDS,)), dma((4,)),
         ],
         compiler_params=pltpu.CompilerParams(
             collective_id=0, has_side_effects=True, vmem_limit_bytes=VMEM_LIMIT

time: 81.6 us -> 80.7 us (0.989)
    pallas_call x1, Pallas kernels: 78.1 us -> 77.3 us  [local(): pl.pallas_call(kernel, out_shape=(jax.ShapeDtypeStruct((TOK, D), bf16), j...]
where the time goes in v4:
time: 80.7 us; the launch traced here: 80.6 us
  Pallas kernels  80 us (99%)
    pallas_call x1, Pallas kernels, local(): pl.pallas_call(kernel, out_shape=(jax.ShapeDtypeStruct((TOK, D), bf16), j...  77.3 us
    pallas_call x1, Pallas kernels, local(): pl.pallas_call(flush, out_shape=(jax.ShapeDtypeStruct((TOK, D), bf16), ja...  2.72 us

profile of v4, /device:TPU:1, one launch (start us, length us, event | category | flops | bytes accessed | tf_op | source)
XLA Modules:
  0.0 80.6 jit_solution(1072821205834196196)
XLA Ops:
  0.6 77.3 %demo_step.1 = (bf16[256,8192]{1,0:T(8,128)(2,1)S(1)}, f32[512,512]{1,0:T(8,128)S(1)}, f32[512,512]{1,0:T(8,128)S(1)}) custom-call(bf16[256,8192]{1,0:T(8,128)(2,1)} %x_ref.1, bf16[256,512]{1,0:T(8,128)(2,1)} %c_ref.1, bf16[512,512]{1,0:T(8,128)(2,1)} %w_ref.1, f32[1,512,512]{2,1,0:T(8,128)} %m_ref.1, s32[1,512,256]{2,1,0:T(8,128)} %s_ref.1), custom_call_target="tpu_custom_call" | custom-call | tf_op jit(solution)/shard_map/demo_step/pallas_call | solution.py:436
  77.9 2.7 %flush.1 = (bf16[256,8192]{1,0:T(8,128)(2,1)}, f32[1,512,512]{2,1,0:T(8,128)}, f32[512,512]{1,0:T(8,128)}) custom-call(bf16[256,8192]{1,0:T(8,128)(2,1)S(1)} %get-tuple-element.6.ig_ref, f32[512,512]{1,0:T(8,128)S(1)} %get-tuple-element.7.nm_ref, f32[512,512]{1,0:T(8,128)S(1)} %get-tuple-element.8.u_ref), custom_call_target="tpu_custom_call" | custom-call | tf_op jit(solution)/shard_map/flush/pallas_call | solution.py:473

commit v5 on v4

--- a/solution.py
+++ b/solution.py
@@ -104,7 +104,7 @@
         pl.semaphore_signal(barrier, inc=1, device_id=peer, device_id_type=MESH)
     pl.semaphore_wait(barrier, len(peers))
 
-    c_send = send(c_ref, cb.at[pl.ds(TOK, TOK)], x_ss.at[32], x_rs.at[32], x_mate)
+    c_send = send(c_ref, cb.at[pl.ds(TOK, TOK)], x_ss.at[1], x_rs.at[32], x_mate)
     c_send.start()
 
     def column(half, i):
@@ -113,7 +113,7 @@
 
     def x_send(i):
         return send(
-            x_ref.at[:, pl.ds(column(1 - xl, i), SUB)], xb.at[i, pl.ds(TOK, TOK)], x_ss.at[i], x_rs.at[i], x_mate
+            x_ref.at[:, pl.ds(column(1 - xl, i), SUB)], xb.at[i, pl.ds(TOK, TOK)], x_ss.at[0], x_rs.at[i], x_mate
         )
 
     def x_load(i):
@@ -136,7 +136,7 @@
 
     def plane(k, n):
         slot = wg.at[xl, (z + 8 - n) % 8, piece]
-        return send(w_src if n == 0 else slot, slot, wb_ss.at[k, n], wb_rs.at[k, n], in_plane[k])
+        return send(w_src if n == 0 else slot, slot, wb_ss.at[k], wb_rs.at[k], in_plane[k])
 
     def pass_on(way, s):
         ring(way, s).wait_recv()
@@ -192,11 +192,11 @@
 
     def product(i):
         pltpu.make_async_copy(x_ref.at[:, pl.ds(0, SUB)], xb.at[i, pl.ds(0, TOK)], x_ls.at[i]).wait()
-        send(xb.at[i, pl.ds(0, TOK)], xb.at[i, pl.ds(TOK, TOK)], x_ss.at[i], x_rs.at[i], x_mate).wait_recv()
+        send(xb.at[i, pl.ds(0, TOK)], xb.at[i, pl.ds(TOK, TOK)], x_ss.at[0], x_rs.at[i], x_mate).wait_recv()
         return lax.dot_general(xb[i], cb[...], (((0,), (0,)), ((), ())), preferred_element_type=f32)
 
     def z_copy(way, m):
-        return send(zs.at[way, m], zr.at[way, m], z_ss.at[way, m], z_rs.at[way, m], z_to[way])
+        return send(zs.at[way, m], zr.at[way, m], z_ss.at[0], z_rs.at[way, m], z_to[way])
 
     def step(way, m, i, before):
         total = product(i)
@@ -263,11 +263,16 @@
 
     def pieces(q, k):
         to = ((xh + k // 4) % 2) * 4 + (y + k) % 4
-        return send(pr.at[piece_of(q, to)], rb.at[own_piece[q]], g_ss.at[q, k - 1], g_rs.at[q, k - 1], chips[k])
+        return send(pr.at[piece_of(q, to)], rb.at[own_piece[q]], g_ss.at[q], g_rs.at[q], chips[k])
 
     def shares(q, k):
         at = sb.at[own_piece[q], mine]
-        return send(at, at, h_ss.at[q, k - 1], h_rs.at[q, k - 1], chips[k])
+        return send(at, at, h_ss.at[q], h_rs.at[q], chips[k])
+
+    def seven(q, ss, rs):
+        first, count = ROUNDS[q]
+        at = pr.at[pl.ds(first * SUB, 7 * (count * SUB // 8))]
+        return send(at, at, ss.at[q], rs.at[q], chips[1])
 
     def halves(q):
         at = sb.at[span[q], mine]
@@ -299,15 +304,13 @@
 
     def gather(q):
         rb[own_piece[q], :] = pr[own_piece[q], :]
-        for k in range(1, 8):
-            pieces(q, k).wait_recv()
+        seven(q, g_ss, g_rs).wait_recv()
         sb[own_piece[q], mine] = jnp.sum(rb[span[q], :].astype(f32).reshape(8, -1, TILE), axis=0).astype(bf16)
         for k in FAR:
             shares(q, k).start()
 
     def exchange(q):
-        for k in range(1, 8):
-            shares(q, k).wait_recv()
+        seven(q, h_ss, h_rs).wait_recv()
         halves(q).start()
 
     def result(q):
@@ -329,9 +332,9 @@
     steps(3)
     input_grad(0)
     steps(4)
-    for k in range(3):
-        for n in range(8):
-            plane(k, n).wait_recv()
+    eight = [send(group(xl, y, c), group(xl, y, c), wb_ss.at[k], wb_rs.at[k], in_plane[k]) for k in range(3)]
+    for copy in eight:
+        copy.wait_recv()
     for k in (2, 3, 1):
         wd[k].start()
     for k in (3, 1, 2):
@@ -371,15 +374,14 @@
     wc[7].start()
     gather(0)
     c_send.wait_send()
-    for i in range(32):
-        x_send(i).wait_send()
+    sent = xb.at[:, pl.ds(0, TOK)]
+    send(sent, sent, x_ss.at[0], x_rs.at[0], x_mate).wait_send()
     for s in range(4):
         ring(0, s).wait_send()
     for s in range(3):
         ring(1, s).wait_send()
-    for k in range(3):
-        for n in range(8):
-            plane(k, n).wait_send()
+    for copy in eight:
+        copy.wait_send()
     input_grad(6)
     renew(0)
     gather(1)
@@ -387,12 +389,7 @@
     gather(2)
     renew(2)
 
-    def drain(m, carry):
-        z_copy(0, m).wait_send()
-        z_copy(1, m).wait_send()
-        return carry
-
-    lax.fori_loop(0, 14, drain, 0)
+    send(zs, zr, z_ss.at[0], z_rs.at[0, 0], z_to[0]).wait_send()
     for copy in wd:
         copy.wait_send()
     exchange(0)
@@ -402,18 +399,14 @@
         copy.wait_send()
     for q in range(N_ROUNDS):
         pair(q).wait_send()
-        for k in range(1, 8):
-            pieces(q, k).wait_send()
+        seven(q, g_ss, g_rs).wait_send()
     exchange(1)
     result(0)
-    for k in range(1, 8):
-        shares(0, k).wait_send()
-    for k in range(1, 8):
-        shares(1, k).wait_send()
+    seven(0, h_ss, h_rs).wait_send()
+    seven(1, h_ss, h_rs).wait_send()
     exchange(2)
     result(1)
-    for k in range(1, 8):
-        shares(2, k).wait_send()
+    seven(2, h_ss, h_rs).wait_send()
     result(2)
     for q in range(N_ROUNDS):
         halves(q).wait_send()
@@ -458,11 +451,11 @@
             pltpu.VMEM((KW, KW), bf16),
             pltpu.VMEM((2, TILE, TILE), bf16),
             pltpu.VMEM((2, TILE, TILE), bf16),
-            dma((33,)), dma((33,)), dma((32,)),
-            dma((2, 14)), dma((2, 14)),
-            dma((2, 4)), dma((2, 4)), dma((3, 8)), dma((3, 8)), dma((6,)), dma((6,)), dma((8,)), dma((8,)),
+            dma((2,)), dma((33,)), dma((32,)),
+            dma((1,)), dma((2, 14)),
+            dma((2, 4)), dma((2, 4)), dma((3,)), dma((3,)), dma((6,)), dma((6,)), dma((8,)), dma((8,)),
             dma((N_ROUNDS,)), dma((N_ROUNDS,)),
-            dma((N_ROUNDS, 7)), dma((N_ROUNDS, 7)), dma((N_ROUNDS, 7)), dma((N_ROUNDS, 7)),
+            dma((N_ROUNDS,)), dma((N_ROUNDS,)), dma((N_ROUNDS,)), dma((N_ROUNDS,)),
             dma((N_ROUNDS,)), dma((N_ROUNDS,)), dma((4,)),
         ],
         compiler_params=pltpu.CompilerParams(

time: 80.7 us -> 79.2 us (0.981)
  Pallas kernels: 80 us -> 78.5 us
    pallas_call x1, Pallas kernels: 77.3 us -> 75.7 us  [local(): pl.pallas_call(kernel, out_shape=(jax.ShapeDtypeStruct((TOK, D), bf16), j...]
where the time goes in v5:
time: 79.2 us; the launch traced here: 79.1 us
  Pallas kernels  78.5 us (99%)
    pallas_call x1, Pallas kernels, local(): pl.pallas_call(kernel, out_shape=(jax.ShapeDtypeStruct((TOK, D), bf16), j...  75.7 us
    pallas_call x1, Pallas kernels, local(): pl.pallas_call(flush, out_shape=(jax.ShapeDtypeStruct((TOK, D), bf16), ja...  2.72 us

profile of v5, /device:TPU:1, one launch (start us, length us, event | category | flops | bytes accessed | tf_op | source)
XLA Modules:
  0.0 79.1 jit_solution(17251460251239942454)
XLA Ops:
  0.6 75.7 %demo_step.1 = (bf16[256,8192]{1,0:T(8,128)(2,1)S(1)}, f32[512,512]{1,0:T(8,128)S(1)}, f32[512,512]{1,0:T(8,128)S(1)}) custom-call(bf16[256,8192]{1,0:T(8,128)(2,1)} %x_ref.1, bf16[256,512]{1,0:T(8,128)(2,1)} %c_ref.1, bf16[512,512]{1,0:T(8,128)(2,1)} %w_ref.1, f32[1,512,512]{2,1,0:T(8,128)} %m_ref.1, s32[1,512,256]{2,1,0:T(8,128)} %s_ref.1), custom_call_target="tpu_custom_call" | custom-call | tf_op jit(solution)/shard_map/demo_step/pallas_call | solution.py:429
  76.4 2.7 %flush.1 = (bf16[256,8192]{1,0:T(8,128)(2,1)}, f32[1,512,512]{2,1,0:T(8,128)}, f32[512,512]{1,0:T(8,128)}) custom-call(bf16[256,8192]{1,0:T(8,128)(2,1)S(1)} %get-tuple-element.6.ig_ref, f32[512,512]{1,0:T(8,128)S(1)} %get-tuple-element.7.nm_ref, f32[512,512]{1,0:T(8,128)S(1)} %get-tuple-element.8.u_ref), custom_call_target="tpu_custom_call" | custom-call | tf_op jit(solution)/shard_map/flush/pallas_call | solution.py:466
